TPU v7x, 256 devices: a whole 4x4x8 slice. The times are simulated.
256 devices in a mesh: row: 16 (over z, y_hi), col: 16 (over y_lo, x, core).
Axes of the slice: x: 4, y: 4 (y_hi: 2, y_lo: 2; y = y_hi * 2 + y_lo), z: 8, core: 2. Of those that a mesh axis runs over, the one named last changes fastest.
Arguments:
- object_field: float32 [2, 8192, 8192], P(None, 'row', 'col'), may hold values from -6 to 6
- probe: float32 [2, 256, 256], replicated, may hold values from -5 to 5
- positions: int32 [512, 2], P(('row', 'col')), may hold values from 0 to 8191, as said below
- amplitudes: float32 [512, 256, 256], P(('row', 'col')), may hold values from 0 to 3
- counts: int32 [256], P(('row', 'col')), may hold values from 1 to 2, as said below
Outputs:
- object_grad: float32 [2, 8192, 8192], P(None, 'row', 'col')
- probe_grad: float32 [2, 256, 256], replicated
Inputs may be any that keep to these rules, and one draw needn't show every extreme that they name: Every slot's window starts inside the tile of the device that holds the slot: positions of slot s lie in tile s div 2, numbered row by row over 16 x 16 tiles. `counts`: some tile has exactly 2 live slots.
All inputs are finite; a program needn't handle non-finite values.
Results may differ from a plain program's by a relative error of at most 0.0003.
Values sent between devices are 32-bit elements; how exact they have to be, the bound alone decides.
No kernel may reach another device: no remote copies, remote signals or barrier semaphores. Data moves between devices by JAX's collectives and lax.ppermute only.
A program may use at most 64 MiB of HBM per device.

v0:
```python
import math

import jax
import jax.numpy as jnp
from jax import lax
from jax.sharding import PartitionSpec as P


def shifted(block, axis, distance):
    devices = range(lax.axis_size(axis))
    route = [(i - distance, i) for i in devices if i - distance in devices]
    return lax.ppermute(block, axis, route)


def dft_tables(window):
    phases_int = lax.broadcasted_iota(jnp.int32, (window, window), 0) * lax.broadcasted_iota(
        jnp.int32, (window, window), 1
    )
    phases = (phases_int % window).astype(jnp.float32) * (2.0 * math.pi / window)
    norm_scale = 1.0 / math.sqrt(window)
    return (jnp.cos(phases) * norm_scale, -jnp.sin(phases) * norm_scale)


def matmul(first, second):
    return jnp.dot(
        first, second, precision=lax.Precision.HIGHEST, preferred_element_type=jnp.float32
    )


def transform(real_part, imag_part, cos_table, sin_table):
    left_re = matmul(cos_table, real_part) - matmul(sin_table, imag_part)
    left_im = matmul(cos_table, imag_part) + matmul(sin_table, real_part)
    out_re = matmul(left_re, cos_table) - matmul(left_im, sin_table)
    out_im = matmul(left_im, cos_table) + matmul(left_re, sin_table)
    return (out_re, out_im)


def position_terms(patch_field, measured, probe, cos_table, sin_table, sin_back):
    patch_re = patch_field[0]
    patch_im = patch_field[1]
    probe_re = probe[0]
    probe_im = probe[1]
    wave_re = probe_re * patch_re - probe_im * patch_im
    wave_im = probe_re * patch_im + probe_im * patch_re
    far_re, far_im = transform(wave_re, wave_im, cos_table, sin_table)
    factor = 1.0 - measured / jnp.sqrt(far_re * far_re + far_im * far_im + 1.0)
    back_re, back_im = transform(factor * far_re, factor * far_im, cos_table, sin_back)
    object_term = jnp.stack(
        [probe_re * back_re + probe_im * back_im, probe_re * back_im - probe_im * back_re]
    )
    probe_term = jnp.stack(
        [patch_re * back_re + patch_im * back_im, patch_re * back_im - patch_im * back_re]
    )
    return (object_term, probe_term)


def shards(object_field, probe, positions, amplitudes, counts):
    tile_size = object_field.shape[1]
    window = probe.shape[1]
    cos_table, sin_table = dft_tables(window)
    sin_back = -sin_table
    right_strip = shifted(object_field[:, :, :window], "col", -1)
    wide_field = jnp.concatenate([object_field, right_strip], axis=2)
    below_strip = shifted(wide_field[:, :window, :], "row", -1)
    extended = jnp.concatenate([wide_field, below_strip], axis=1)
    offsets = positions % tile_size
    live_count = counts[0]

    def own_step(slot_index, state_pair):
        grad_ext, grad_probe = state_pair
        row_start = offsets[slot_index, 0]
        col_start = offsets[slot_index, 1]
        patch_field = lax.dynamic_slice(extended, (0, row_start, col_start), (2, window, window))
        measured = lax.dynamic_index_in_dim(amplitudes, slot_index, 0, keepdims=False)
        object_term, probe_term = position_terms(
            patch_field, measured, probe, cos_table, sin_table, sin_back
        )
        current = lax.dynamic_slice(grad_ext, (0, row_start, col_start), (2, window, window))
        grad_ext = lax.dynamic_update_slice(
            grad_ext, current + object_term, (0, row_start, col_start)
        )
        return (grad_ext, grad_probe + probe_term)

    initial = (jnp.zeros_like(extended), jnp.zeros((2, window, window), jnp.float32))
    grad_ext, grad_probe = lax.fori_loop(0, live_count, own_step, initial)
    from_above = shifted(grad_ext[:, tile_size:, :], "row", 1)
    wide_grad = grad_ext[:, :tile_size, :].at[:, :window, :].add(from_above)
    from_left = shifted(wide_grad[:, :, tile_size:], "col", 1)
    tile_grad = wide_grad[:, :, :tile_size].at[:, :, :window].add(from_left)
    probe_total = lax.psum(grad_probe, ("row", "col"))
    return (tile_grad, probe_total)


def solution(mesh):
    return jax.shard_map(
        shards,
        mesh=mesh,
        in_specs=(
            P(None, "row", "col"),
            P(),
            P(("row", "col"), None),
            P(("row", "col"), None, None),
            P(("row", "col")),
        ),
        out_specs=(P(None, "row", "col"), P()),
        check_vma=False,
    )
```

profile of v0, /device:TPU:1, one launch (start us, length us, event | category | flops | bytes accessed | tf_op | source)
XLA Modules:
  0.0 465.2 jit_solution(7605001895915374066)
XLA Ops:
  8.7 5.1 %collective-permute-start = (f32[2,512,256]{2,1,0:T(8,128)S(1)}, f32[2,512,256]{2,1,0:T(8,128)S(1)}, u32[]{:S(2)}, u32[]{:S(2)}) collective-permute-start(f32[2,512,256]{2,1,0:T(8,128)S(1)} %slice.80), channel_id=1, source_target_pairs={{1,0},{2,1},{3,2},{4,3},{5,4},{6,5},{7,6},{8,7},{9,8},{10,9},{11,1... | collective-permute-start | bytes 3145736 | tf_op jit(solution)/shard_map/ppermute | solution.py:12
  14.0 11.6 %collective-permute-done = f32[2,512,256]{2,1,0:T(8,128)S(1)} collective-permute-done((f32[2,512,256]{2,1,0:T(8,128)S(1)}, f32[2,512,256]{2,1,0:T(8,128)S(1)}, u32[]{:S(2)}, u32[]{:S(2)}) %collective-permute-start) | collective-permute-done | bytes 1048608 | tf_op jit(solution)/shard_map/ppermute | solution.py:12
  25.7 1.6 copy-done.3
  29.9 29.7 %collective-permute-done.1 = f32[2,256,768]{2,1,0:T(8,128)S(1)} collective-permute-done((f32[2,256,768]{2,1,0:T(8,128)}, f32[2,256,768]{2,1,0:T(8,128)S(1)}, u32[]{:S(2)}, u32[]{:S(2)}) %collective-permute-start.1) | collective-permute-done | bytes 1572896 | tf_op jit(solution)/shard_map/ppermute | solution.py:12
  59.6 4.3 pad_maximum_fusion
  63.9 2.5 broadcast_in_dim.6
  66.4 39.7 %while.16 = (s32[]{:T(128)}, f32[2,768,768]{2,1,0:T(8,128)}, f32[2,256,256]{2,1,0:T(8,128)S(1)}, s32[]{:T(128)}, s32[2,2]{1,0:T(2,128)S(1)}, /*index=5*/f32[2,25...) while((s32[]{:T(128)}, f32[2,768,768]{2,1,0:T(8,128)}, ...), condition=%wide.region_1.2_spmd.clone.clone, body=%wide.region_0.1_spmd.clone.clone.sunk | while | flops 3240493056 | bytes 19136820 | solution.py:85
  83.1 1.5 fusion.188
  86.1 1.5 convolution_add_fusion.8
  89.1 1.5 convolution_subtract_fusion.9
  95.0 2.7 add_bitcast_fusion.2
  97.7 1.5 maximum_add_fusion.3
  99.2 6.3 %dynamic_update_slice.6 = f32[2,768,768]{2,1,0:T(8,128)} dynamic-update-slice(f32[2,768,768]{2,1,0:T(8,128)} %get-tuple-element.308, f32[2,256,256]{2,1,0:T(8,128)S(1)} %get-tuple-element.292, s32[]{:T(128)} %constant.94.clone.1..sunk, s32[]{:T(128)S(6)} %select_n.153, s32[]{:T(128)S(6)} %select_n.154) | dynamic-update-slice | bytes 1048580 | tf_op jit(solution)/shard_map/while/body/dynamic_update_slice | solution.py:79
  106.2 1.7 slice.84
  107.9 4.6 collective-permute-start.2
  112.5 2.1 slice.82
  114.6 22.1 %collective-permute-done.2 = f32[2,256,768]{2,1,0:T(8,128)S(1)} collective-permute-done((f32[2,256,768]{2,1,0:T(8,128)S(1)}, f32[2,256,768]{2,1,0:T(8,128)S(1)}, u32[]{:S(2)}, u32[]{:S(2)}) %collective-permute-start.2) | collective-permute-done | bytes 1572896 | tf_op jit(solution)/shard_map/ppermute | solution.py:12
  136.7 1.7 add_dynamic-update-slice_fusion
  138.4 1.6 copy-done.2
  141.0 22.7 %collective-permute-start.3 = (f32[2,512,256]{2,1,0:T(8,128)}, f32[2,512,256]{2,1,0:T(8,128)S(1)}, u32[]{:S(2)}, u32[]{:S(2)}) collective-permute-start(f32[2,512,256]{2,1,0:T(8,128)} %slice.99), channel_id=1, source_target_pairs={{0,1},{1,2},{2,3},{3,4},{4,5},{5,6},{6,7},{7,8},{8,9},{9,10},{10,1... | collective-permute-start | bytes 3145736 | tf_op jit(solution)/shard_map/ppermute | solution.py:12
  163.7 1.8 slice.97
  165.5 10.2 %collective-permute-done.3 = f32[2,512,256]{2,1,0:T(8,128)S(1)} collective-permute-done((f32[2,512,256]{2,1,0:T(8,128)}, f32[2,512,256]{2,1,0:T(8,128)S(1)}, u32[]{:S(2)}, u32[]{:S(2)}) %collective-permute-start.3) | collective-permute-done | bytes 1048608 | tf_op jit(solution)/shard_map/ppermute | solution.py:12
  177.2 279.3 %all-reduce.2.cloned.1.call-done = f32[2,256,256]{2,1,0:T(8,128)} async-done(((f32[2,256,256]{2,1,0:T(8,128)}), f32[2,256,256]{2,1,0:T(8,128)}) %all-reduce.2.cloned.1.call-update) | async-done | bytes 524304 | tf_op jit(solution)/shard_map/psum | solution.py:90
  456.4 1.9 copy.21
  (39 shorter events, 26.3 us)
Async XLA Ops:
  7.2 6.7 %copy-start.4 = (f32[2,512,512]{2,1,0:T(8,128)S(1)}, f32[2,512,512]{2,1,0:T(8,128)}, u32[]{:S(2)}) copy-start(f32[2,512,512]{2,1,0:T(8,128)} %param.11) | copy-start | bytes 6291460
  7.2 449.3 %all-reduce.2.cloned.1.call-start = ((), (), s32[]{:S(2)}) async-start(), calls=%async_computation | async-start | bytes 1048576 | tf_op jit(solution)/shard_map/psum | solution.py:90
  8.7 17.0 %collective-permute-start = (f32[2,512,256]{2,1,0:T(8,128)S(1)}, f32[2,512,256]{2,1,0:T(8,128)S(1)}, u32[]{:S(2)}, u32[]{:S(2)}) collective-permute-start(f32[2,512,256]{2,1,0:T(8,128)S(1)} %slice.80), channel_id=1, source_target_pairs={{1,0},{2,1},{3,2},{4,3},{5,4},{6,5},{7,6},{8,7},{9,8},{10,9},{11,1... | collective-permute-start | bytes 3145736 | tf_op jit(solution)/shard_map/ppermute | solution.py:12
  14.0 15.9 %copy-start.6 = (s32[2,2]{1,0:T(2,128)S(1)}, s32[2,2]{1,0:T(2,128)}, u32[]{:S(2)}) copy-start(s32[2,2]{1,0:T(2,128)} %param.13) | copy-start | bytes 52
  25.7 1.6 copy-start.3
  28.6 31.0 %collective-permute-start.1 = (f32[2,256,768]{2,1,0:T(8,128)}, f32[2,256,768]{2,1,0:T(8,128)S(1)}, u32[]{:S(2)}, u32[]{:S(2)}) collective-permute-start(f32[2,256,768]{2,1,0:T(8,128)} %slice.96), channel_id=1, source_target_pairs={{16,0},{32,16},{48,32},{64,48},{80,64},{96,80},{112,96},{128,112},... | collective-permute-start | bytes 4718600 | tf_op jit(solution)/shard_map/ppermute | solution.py:12
  63.9 2.5 copy-start
  63.9 2.5 copy-start.7
  106.1 8.5 %copy-start.1 = (f32[2,256,256]{2,1,0:T(8,128)}, f32[2,256,256]{2,1,0:T(8,128)S(1)}, u32[]{:S(2)}) copy-start(f32[2,256,256]{2,1,0:T(8,128)S(1)} %get-tuple-element.125) | copy-start | bytes 1572868
  107.9 28.8 %collective-permute-start.2 = (f32[2,256,768]{2,1,0:T(8,128)S(1)}, f32[2,256,768]{2,1,0:T(8,128)S(1)}, u32[]{:S(2)}, u32[]{:S(2)}) collective-permute-start(f32[2,256,768]{2,1,0:T(8,128)S(1)} %slice.84), channel_id=1, source_target_pairs={{0,16},{16,32},{32,48},{48,64},{64,80},{80,96},{96,112},{112,128},... | collective-permute-start | bytes 4718600 | tf_op jit(solution)/shard_map/ppermute | solution.py:12
  138.4 1.6 copy-start.2
  141.0 34.7 %collective-permute-start.3 = (f32[2,512,256]{2,1,0:T(8,128)}, f32[2,512,256]{2,1,0:T(8,128)S(1)}, u32[]{:S(2)}, u32[]{:S(2)}) collective-permute-start(f32[2,512,256]{2,1,0:T(8,128)} %slice.99), channel_id=1, source_target_pairs={{0,1},{1,2},{2,3},{3,4},{4,5},{5,6},{6,7},{7,8},{8,9},{9,10},{10,1... | collective-permute-start | bytes 3145736 | tf_op jit(solution)/shard_map/ppermute | solution.py:12
  177.2 281.1 %copy-start.5 = (f32[2,512,512]{2,1,0:T(8,128)}, f32[2,512,512]{2,1,0:T(8,128)S(1)}, u32[]{:S(2)}) copy-start(f32[2,512,512]{2,1,0:T(8,128)S(1)} %fusion.113) | copy-start | bytes 6291460
Sparse Core Ops, SparseCore 0:
  163.9 292.5 all-reduce.1
where the time goes:
time: 466 us; the launch traced here: 465 us
  waiting for transfers between devices  353 us (76%)
  starting transfers between devices  33.8 us (7%)
  matrix products  24.8 us (5%)
  local copies, waits for them, and re-layouts  24 us (5%)
  between operations  14.2 us (3%)
  other arithmetic  10.3 us (2%)
  loops' own time  5.25 us (1%)
    psum x1, waiting for transfers between devices, shards(): probe_total = lax.psum(grad_probe, ('row', 'col'))  279 us
    ppermute x4, waiting for transfers between devices, shifted(): return lax.ppermute(block, axis, route)  73.6 us
    ppermute x4, starting transfers between devices, shifted(): return lax.ppermute(block, axis, route)  33.7 us
    dot_general x16, matrix products, matmul(): jnp.dot(first, second, precision=lax.Precision.HIGHEST, preferred_element...  24.8 us
  transfers between devices with their start and end apart: 5, of which 5 were waited for; matrix products, arithmetic and copies ran while one was open for 1% of the time, Pallas kernels for 0%

commit v1 on v0

v1 whole, which is shorter than its diff:
```python
import functools
import math

import jax
import jax.numpy as jnp
import ml_dtypes
import numpy as np
from jax import lax
from jax.experimental import pallas as pl
from jax.experimental.pallas import tpu as pltpu
from jax.sharding import PartitionSpec as P

AXES = ("row", "col")
ANY = pl.BlockSpec(memory_space=pl.ANY)
SMEM = pl.BlockSpec(memory_space=pltpu.SMEM)
VMEM = pl.BlockSpec(memory_space=pltpu.VMEM)
MIB = 1024 * 1024
SIZES = {"x": 4, "y": 4, "z": 8, "core": 2}


def shifted(block, axis, distance):
    devices = range(lax.axis_size(axis))
    route = [(i - distance, i) for i in devices if i - distance in devices]
    return lax.ppermute(block, axis, route)


def dft_tables(window):
    index = np.arange(window)
    phases = (np.outer(index, index) % window) * (2.0 * math.pi / window)
    re, im = np.cos(phases) / math.sqrt(window), -np.sin(phases) / math.sqrt(window)
    table = np.block([[re, im], [-im, re]])
    high = table.astype(ml_dtypes.bfloat16)
    low = (table - high.astype(np.float64)).astype(ml_dtypes.bfloat16)
    return high, low, high.T.copy(), low.T.copy()


def probe_kernel(window, tile, pos_ref, probe_ref, out_ref):
    for slot in range(out_ref.shape[0]):
        row = lax.rem(lax.rem(pos_ref[slot, 0], tile), window)
        col = lax.rem(lax.rem(pos_ref[slot, 1], tile), window)
        for plane in range(2):
            turned = pltpu.roll(probe_ref[plane], row, 0)
            out_ref[slot, plane] = pltpu.roll(turned, col, 1)


def turned_probe(positions, probe, tile):
    slots, window = positions.shape[0], probe.shape[1]
    return pl.pallas_call(
        functools.partial(probe_kernel, window, tile),
        out_shape=jax.ShapeDtypeStruct((slots, 2, window, window), jnp.float32),
        in_specs=[SMEM, VMEM],
        out_specs=VMEM,
        cost_estimate=pl.CostEstimate(flops=4000000, bytes_accessed=2 * MIB, transcendentals=0),
        name="turned_probe",
    )(positions, probe)


def split(value):
    high = value.astype(jnp.bfloat16)
    return high, (value - high.astype(jnp.float32)).astype(jnp.bfloat16)


def dot(first, second):
    return jnp.dot(first, second, preferred_element_type=jnp.float32)


def dot_right(value, high_ref, low_ref):
    high, low = split(value)
    return dot(high, high_ref[...]) + (dot(low, high_ref[...]) + dot(high, low_ref[...]))


def dot_left(high_ref, low_ref, value):
    high, low = split(value)
    return dot(high_ref[...], high) + (dot(high_ref[...], low) + dot(low_ref[...], high))


def slots_kernel(
    window, tile,
    counts_ref, pos_ref, object_hbm, right_hbm, below0_hbm, below1_hbm, corner_hbm,
    turned_hbm, amp_hbm, high_hbm, low_hbm, thigh_hbm, tlow_hbm,
    tile_out, right_out, below0_out, below1_out, corner_out, probe_out,
    ext, grad, turned, amp, high, low, thigh, tlow, patch, probe_grad, sems,
):
    w, t = window, tile
    e = t + w
    moves = [
        (object_hbm, ext.at[:, 0:t, 0:t]),
        (right_hbm, ext.at[:, 0:t, t:e]),
        (below0_hbm, ext.at[:, t:e, 0:w]),
        (below1_hbm, ext.at[:, t:e, w:t]),
        (corner_hbm, ext.at[:, t:e, t:e]),
        (turned_hbm, turned),
        (amp_hbm, amp),
        (high_hbm, high),
        (low_hbm, low),
        (thigh_hbm, thigh),
        (tlow_hbm, tlow),
    ]
    copies = [pltpu.make_async_copy(a, b, sems.at[i]) for i, (a, b) in enumerate(moves)]
    for copy in copies:
        copy.start()
    grad[...] = jnp.zeros_like(grad)
    probe_grad[...] = jnp.zeros_like(probe_grad)
    for copy in copies:
        copy.wait()
    rows = lax.broadcasted_iota(jnp.int32, (w, w), 0)
    cols = lax.broadcasted_iota(jnp.int32, (w, w), 1)

    def one_slot(slot, carry):
        top = lax.rem(pos_ref[slot, 0], t)
        left = lax.rem(pos_ref[slot, 1], t)
        row_turn, col_turn = lax.rem(top, w), lax.rem(left, w)
        row_at = pl.multiple_of((top // w) * w, w)
        col_at = pl.multiple_of((left // w) * w, w)
        in_low = rows < row_turn
        in_right = cols < col_turn
        blocks = [
            (pl.ds(row_at, w), pl.ds(col_at, w), ~in_low & ~in_right),
            (pl.ds(row_at, w), pl.ds(col_at + w, w), ~in_low & in_right),
            (pl.ds(row_at + w, w), pl.ds(col_at, w), in_low & ~in_right),
            (pl.ds(row_at + w, w), pl.ds(col_at + w, w), in_low & in_right),
        ]
        for plane in range(2):
            upper = jnp.where(
                in_right, ext[plane, blocks[1][0], blocks[1][1]], ext[plane, blocks[0][0], blocks[0][1]]
            )
            lower = jnp.where(
                in_right, ext[plane, blocks[3][0], blocks[3][1]], ext[plane, blocks[2][0], blocks[2][1]]
            )
            patch[plane] = jnp.where(in_low, lower, upper)
        probe_re, probe_im = turned[slot, 0], turned[slot, 1]
        wave = jnp.concatenate(
            [probe_re * patch[0] - probe_im * patch[1], probe_re * patch[1] + probe_im * patch[0]], axis=1
        )
        half = dot_right(wave, high, low)
        half = jnp.concatenate([half[:, :w], half[:, w:]], axis=0)
        far = dot_left(thigh, tlow, half)
        far_re, far_im = far[:w], far[w:]
        factor = 1.0 - amp[slot] / jnp.sqrt(far_re * far_re + far_im * far_im + 1.0)
        wave = jnp.concatenate([factor * far_re, factor * far_im], axis=1)
        half = dot_right(wave, thigh, tlow)
        half = jnp.concatenate([half[:, :w], half[:, w:]], axis=0)
        back = dot_left(high, low, half)
        back_re, back_im = back[:w], back[w:]
        terms = (
            turned[slot, 0] * back_re + turned[slot, 1] * back_im,
            turned[slot, 0] * back_im - turned[slot, 1] * back_re,
        )
        for at_rows, at_cols, mask in blocks:
            for plane in range(2):
                grad[plane, at_rows, at_cols] += jnp.where(mask, terms[plane], 0.0)
        terms = (patch[0] * back_re + patch[1] * back_im, patch[0] * back_im - patch[1] * back_re)
        for plane in range(2):
            term = pltpu.roll(terms[plane], lax.rem(w - row_turn, w), 0)
            probe_grad[plane] += pltpu.roll(term, lax.rem(w - col_turn, w), 1)
        return carry

    lax.fori_loop(0, counts_ref[0], one_slot, 0)
    moves = [
        (probe_grad, probe_out),
        (grad.at[:, t:e, t:e], corner_out),
        (grad.at[:, t:e, w:t], below1_out),
        (grad.at[:, t:e, 0:w], below0_out),
        (grad.at[:, 0:t, t:e], right_out),
        (grad.at[:, 0:t, 0:t], tile_out),
    ]
    copies = [pltpu.make_async_copy(a, b, sems.at[i]) for i, (a, b) in enumerate(moves)]
    for copy in copies:
        copy.start()
    for copy in copies:
        copy.wait()


def slot_terms(counts, positions, object_field, right, below0, below1, corner, turned, amplitudes):
    w, t = below0.shape[1], object_field.shape[1]
    slots = positions.shape[0]
    tables = [jnp.asarray(table) for table in dft_tables(w)]
    f32 = functools.partial(jax.ShapeDtypeStruct, dtype=jnp.float32)
    block = f32((2, w, w))
    return pl.pallas_call(
        functools.partial(slots_kernel, w, t),
        out_shape=[f32((2, t, t)), f32((2, t, w)), block, block, block, block],
        in_specs=[SMEM, SMEM] + [ANY] * 11,
        out_specs=[ANY] * 6,
        scratch_shapes=[
            pltpu.VMEM((2, t + w, t + w), jnp.float32),
            pltpu.VMEM((2, t + w, t + w), jnp.float32),
            pltpu.VMEM((slots, 2, w, w), jnp.float32),
            pltpu.VMEM((slots, w, w), jnp.float32),
            pltpu.VMEM((2 * w, 2 * w), jnp.bfloat16),
            pltpu.VMEM((2 * w, 2 * w), jnp.bfloat16),
            pltpu.VMEM((2 * w, 2 * w), jnp.bfloat16),
            pltpu.VMEM((2 * w, 2 * w), jnp.bfloat16),
            pltpu.VMEM((2, w, w), jnp.float32),
            pltpu.VMEM((2, w, w), jnp.float32),
            pltpu.SemaphoreType.DMA((11,)),
        ],
        compiler_params=pltpu.CompilerParams(vmem_limit_bytes=32 * MIB),
        cost_estimate=pl.CostEstimate(flops=3 * 10**9, bytes_accessed=14 * MIB, transcendentals=0),
        name="slot_terms",
    )(counts, positions, object_field, right, below0, below1, corner, turned, amplitudes, *tables)


def combine_kernel(half, tile_ref, left_ref, above0_ref, above1_ref, out_ref):
    w = left_ref.shape[2]
    first, second = tile_ref[:, :, :w] + left_ref[...], tile_ref[:, :, w:]

    @pl.when(pl.program_id(0) < half)
    def _():
        out_ref[:, :, :w] = first + above0_ref[...]
        out_ref[:, :, w:] = second + above1_ref[...]

    @pl.when(pl.program_id(0) >= half)
    def _():
        out_ref[:, :, :w] = first
        out_ref[:, :, w:] = second


def combined(tile_grad, from_left, above0, above1):
    t, w = tile_grad.shape[1], from_left.shape[2]
    step = w // 2
    half = w // step
    above = pl.BlockSpec((2, step, w), lambda i: (0, jnp.minimum(i, half - 1), 0))
    return pl.pallas_call(
        functools.partial(combine_kernel, half),
        out_shape=jax.ShapeDtypeStruct(tile_grad.shape, jnp.float32),
        grid=(t // step,),
        in_specs=[
            pl.BlockSpec((2, step, t), lambda i: (0, i, 0)),
            pl.BlockSpec((2, step, w), lambda i: (0, i, 0)),
            above,
            above,
        ],
        out_specs=pl.BlockSpec((2, step, t), lambda i: (0, i, 0)),
        cost_estimate=pl.CostEstimate(flops=10**6, bytes_accessed=6 * MIB, transcendentals=0),
        name="combined",
    )(tile_grad, from_left, above0, above1)


def place(x, y, z, core):
    return (z % 8 * 2 + y % 4 // 2) * 16 + y % 2 * 8 + x % 4 * 2 + core % 2


def moved(value, **distance):
    route = []
    for x in range(4):
        for y in range(4):
            for z in range(8):
                for core in range(2):
                    target = place(
                        x + distance.get("x", 0), y + distance.get("y", 0),
                        z + distance.get("z", 0), core + distance.get("core", 0),
                    )
                    route.append((place(x, y, z, core), target))
    return lax.ppermute(value, AXES, route)


def scattered(value, axis, index):
    size = SIZES[axis]
    rows = value.shape[0] // size
    chunk = lambda i: lax.dynamic_slice(value, (i % size * rows, 0), (rows, value.shape[1]))
    parts = [moved(chunk(index + d), **{axis: d}) for d in range(1, size)]
    return functools.reduce(jnp.add, parts, chunk(index))


def summed(value, axis):
    parts = [moved(value, **{axis: d}) for d in range(1, SIZES[axis])]
    return functools.reduce(jnp.add, parts, value)


def gathered(value, axis, index):
    size = SIZES[axis]
    rows = value.shape[0]
    parts = [value] + [moved(value, **{axis: -d}) for d in range(1, size)]
    twice = jnp.concatenate(parts + parts[:-1])
    return lax.dynamic_slice(twice, ((size - index) % size * rows, 0), (size * rows, value.shape[1]))


def total(value):
    if (lax.axis_size("row"), lax.axis_size("col")) != (16, 16):
        return lax.psum(value, AXES)
    shape = value.shape
    row, col = lax.axis_index("row"), lax.axis_index("col")
    z, core = row // 2, col % 2
    value = value.reshape(shape[0] * shape[1], shape[2])
    value = scattered(value, "core", core)
    value = scattered(value, "z", z)
    value = summed(value, "x")
    value = summed(value, "y")
    value = gathered(value, "z", z)
    value = gathered(value, "core", core)
    return value.reshape(shape)


def shards(object_field, probe, positions, amplitudes, counts):
    tile = object_field.shape[1]
    window = probe.shape[1]
    below0 = shifted(object_field[:, :window, :window], "row", -1)
    below1 = shifted(object_field[:, :window, window:], "row", -1)
    right = shifted(object_field[:, :, :window], "col", -1)
    turned = turned_probe(positions, probe, tile)
    corner = shifted(below0, "col", -1)
    tile_grad, right_grad, below0_grad, below1_grad, corner_grad, probe_grad = slot_terms(
        counts, positions, object_field, right, below0, below1, corner, turned, amplitudes
    )
    corner_in = shifted(corner_grad, "col", 1)
    above1 = shifted(below1_grad, "row", 1)
    from_left = shifted(right_grad, "col", 1)
    above0 = shifted(below0_grad + corner_in, "row", 1)
    probe_total = total(probe_grad)
    return combined(tile_grad, from_left, above0, above1), probe_total


def solution(mesh):
    return jax.shard_map(
        shards,
        mesh=mesh,
        in_specs=(
            P(None, "row", "col"),
            P(),
            P(("row", "col"), None),
            P(("row", "col"), None, None),
            P(("row", "col")),
        ),
        out_specs=(P(None, "row", "col"), P()),
        check_vma=False,
    )
```

time: 466 us -> 182 us (0.39)
  the two profiles are of different devices: /device:TPU:1 before, /device:TPU:16 now
where the time goes in v1:
time: 182 us; the launch traced here: 181 us
  starting transfers between devices  71.6 us (39%)
  waiting for transfers between devices  64.9 us (36%)
  local copies, waits for them, and re-layouts  26.2 us (14%)
  Pallas kernels  13.2 us (7%)
  other arithmetic  3.57 us (2%)
    ppermute x22, starting transfers between devices, moved(): return lax.ppermute(value, AXES, route)  50.9 us
    ppermute x22, waiting for transfers between devices, moved(): return lax.ppermute(value, AXES, route)  36.5 us
    ppermute x8, waiting for transfers between devices, shifted(): return lax.ppermute(block, axis, route)  28.4 us
    unnamed x51, local copies, waits for them, and re-layouts  21.3 us
    ppermute x8, starting transfers between devices, shifted(): return lax.ppermute(block, axis, route)  20.7 us
    pallas_call x1, Pallas kernels, slot_terms(): pl.pallas_call(functools.partial(slots_kernel, w, t), out_shape=[f32((2,...  6.49 us
    pallas_call x1, Pallas kernels, combined(): pl.pallas_call(functools.partial(combine_kernel, half), out_shape=jax.Sha...  4.19 us
  transfers between devices with their start and end apart: 30, of which 12 were waited for; matrix products, arithmetic and copies ran while one was open for 7% of the time, Pallas kernels for 1%

profile of v1, /device:TPU:16, one launch (start us, length us, event | category | flops | bytes accessed | tf_op | source)
XLA Modules:
  0.0 181.0 jit_solution(10753945515113100674)
XLA Ops:
  0.6 2.4 %slice.9 = f32[2,512,256]{2,1,0:T(8,128)} slice(f32[2,512,512]{2,1,0:T(8,128)} %object_hbm.1), slice={[0:2], [0:512], [0:256]} | slice | bytes 2097152 | tf_op jit(solution)/shard_map/slice | solution.py:300
  5.4 4.0 %collective-permute-start.1 = (f32[2,256,256]{2,1,0:T(8,128)S(1)}, f32[2,256,256]{2,1,0:T(8,128)}, u32[]{:S(2)}, u32[]{:S(2)}) collective-permute-start(f32[2,256,256]{2,1,0:T(8,128)S(1)} %get-tuple-element.17), channel_id=1, source_target_pairs={{16,0},{32,16},{48,32},{64,48},{80,64},{96,80},{112,96},{128,112},... | collective-permute-start | bytes 1572872 | tf_op jit(solution)/shard_map/ppermute | solution.py:24
  9.4 1.9 %collective-permute-start.2 = (f32[2,256,256]{2,1,0:T(8,128)}, f32[2,256,256]{2,1,0:T(8,128)}, u32[]{:S(2)}, u32[]{:S(2)}) collective-permute-start(f32[2,256,256]{2,1,0:T(8,128)} %get-tuple-element.16), channel_id=1, source_target_pairs={{16,0},{32,16},{48,32},{64,48},{80,64},{96,80},{112,96},{128,112},... | collective-permute-start | bytes 1572872 | tf_op jit(solution)/shard_map/ppermute | solution.py:24
  11.3 13.1 %collective-permute-done.1.below0_hbm = f32[2,256,256]{2,1,0:T(8,128)} collective-permute-done((f32[2,256,256]{2,1,0:T(8,128)S(1)}, f32[2,256,256]{2,1,0:T(8,128)}, u32[]{:S(2)}, u32[]{:S(2)}) %collective-permute-start.1) | collective-permute-done | bytes 524320 | tf_op jit(solution)/shard_map/ppermute | solution.py:24
  26.4 2.5 %turned_probe.1.turned_hbm = f32[2,2,256,256]{3,2,1,0:T(8,128)} custom-call(s32[2,2]{1,0:T(2,128)} %pos_ref.3, f32[2,256,256]{2,1,0:T(8,128)} %probe_ref.1), custom_call_target="tpu_custom_call" | custom-call | flops 4000000 | bytes 2097152 | tf_op jit(solution)/shard_map/turned_probe/pallas_call | solution.py:48
  28.8 6.8 %collective-permute-done.2.below1_hbm = f32[2,256,256]{2,1,0:T(8,128)} collective-permute-done((f32[2,256,256]{2,1,0:T(8,128)}, f32[2,256,256]{2,1,0:T(8,128)}, u32[]{:S(2)}, u32[]{:S(2)}) %collective-permute-start.2) | collective-permute-done | bytes 524320 | tf_op jit(solution)/shard_map/ppermute | solution.py:24
  44.3 6.5 %slot_terms.1 = (f32[2,512,512]{2,1,0:T(8,128)S(1)}, f32[2,512,256]{2,1,0:T(8,128)S(1)}, f32[2,256,256]{2,1,0:T(8,128)S(1)}, f32[2,256,256]{2,1,0:T(8,128)S(1)},...) custom-call(s32[1]{0:T(128)S(6)} %copy.25.counts_ref, s32[2,2]{1,0:T(2,128)S(1)} %copy-done.3, ...), custom_call_target="tpu_custom_call" | custom-call | flops 3000000000 | bytes 14680064 | tf_op jit(solution)/shard_map/slot_terms/pallas_call | solution.py:180
  58.9 6.0 %collective-permute-start.14 = (f32[32,256]{1,0:T(8,128)S(1)}, f32[32,256]{1,0:T(8,128)S(1)}, u32[]{:S(2)}, u32[]{:S(2)}) collective-permute-start(f32[32,256]{1,0:T(8,128)S(1)} %get-tuple-element.20), channel_id=1, source_target_pairs={{0,192},{1,193},{32,224},{33,225},{64,0},{65,1},{96,32},{97,33},{1... | collective-permute-start | bytes 98312 | tf_op jit(solution)/shard_map/ppermute | solution.py:255
  66.2 4.2 %collective-permute-start.12 = (f32[32,256]{1,0:T(8,128)S(1)}, f32[32,256]{1,0:T(8,128)S(1)}, u32[]{:S(2)}, u32[]{:S(2)}) collective-permute-start(f32[32,256]{1,0:T(8,128)S(1)} %get-tuple-element.22), channel_id=1, source_target_pairs={{0,128},{1,129},{32,160},{33,161},{64,192},{65,193},{96,224},{97,2... | collective-permute-start | bytes 98312 | tf_op jit(solution)/shard_map/ppermute | solution.py:255
  70.4 3.7 %collective-permute-start.10 = (f32[32,256]{1,0:T(8,128)S(1)}, f32[32,256]{1,0:T(8,128)S(1)}, u32[]{:S(2)}, u32[]{:S(2)}) collective-permute-start(f32[32,256]{1,0:T(8,128)S(1)} %get-tuple-element.24), channel_id=1, source_target_pairs={{0,64},{1,65},{32,96},{33,97},{64,128},{65,129},{96,160},{97,161},... | collective-permute-start | bytes 98312 | tf_op jit(solution)/shard_map/ppermute | solution.py:255
  74.8 3.0 %collective-permute-done.11 = f32[32,256]{1,0:T(8,128)S(1)} collective-permute-done((f32[32,256]{1,0:T(8,128)S(1)}, f32[32,256]{1,0:T(8,128)S(1)}, u32[]{:S(2)}, u32[]{:S(2)}) %collective-permute-start.11) | collective-permute-done | bytes 32800 | tf_op jit(solution)/shard_map/ppermute | solution.py:255
  79.2 7.6 %collective-permute-start.18 = (f32[32,256]{1,0:T(8,128)S(1)}, f32[32,256]{1,0:T(8,128)S(1)}, u32[]{:S(2)}, u32[]{:S(2)}) collective-permute-start(f32[32,256]{1,0:T(8,128)S(1)} %add_add_fusion.2), channel_id=1, source_target_pairs={{0,6},{1,7},{32,38},{33,39},{64,70},{65,71},{96,102},{97,103},{128... | collective-permute-start | bytes 98312 | tf_op jit(solution)/shard_map/ppermute | solution.py:255
  88.4 3.9 %collective-permute-done.17 = f32[32,256]{1,0:T(8,128)S(1)} collective-permute-done((f32[32,256]{1,0:T(8,128)S(1)}, f32[32,256]{1,0:T(8,128)S(1)}, u32[]{:S(2)}, u32[]{:S(2)}) %collective-permute-start.17) | collective-permute-done | bytes 32800 | tf_op jit(solution)/shard_map/ppermute | solution.py:255
  92.3 11.2 %collective-permute-start.21 = (f32[32,256]{1,0:T(8,128)S(1)}, f32[32,256]{1,0:T(8,128)S(1)}, u32[]{:S(2)}, u32[]{:S(2)}) collective-permute-start(f32[32,256]{1,0:T(8,128)S(1)} %add_add_fusion.1), channel_id=1, source_target_pairs={{0,24},{1,25},{32,56},{33,57},{64,88},{65,89},{96,120},{97,121},{1... | collective-permute-start | bytes 98312 | tf_op jit(solution)/shard_map/ppermute | solution.py:255
  105.7 3.2 %collective-permute-done.20 = f32[32,256]{1,0:T(8,128)S(1)} collective-permute-done((f32[32,256]{1,0:T(8,128)S(1)}, f32[32,256]{1,0:T(8,128)S(1)}, u32[]{:S(2)}, u32[]{:S(2)}) %collective-permute-start.20) | collective-permute-done | bytes 32800 | tf_op jit(solution)/shard_map/ppermute | solution.py:255
  110.0 2.3 %collective-permute-start.4 = (f32[2,512,256]{2,1,0:T(8,128)S(1)}, f32[2,512,256]{2,1,0:T(8,128)}, u32[]{:S(2)}, u32[]{:S(2)}) collective-permute-start(f32[2,512,256]{2,1,0:T(8,128)S(1)} %copy-done.5), channel_id=1, source_target_pairs={{0,1},{1,2},{2,3},{3,4},{4,5},{5,6},{6,7},{7,8},{8,9},{9,10},{10,1... | collective-permute-start | bytes 3145736 | tf_op jit(solution)/shard_map/ppermute | solution.py:24
  114.1 6.1 %collective-permute-start.7 = (f32[2,256,256]{2,1,0:T(8,128)S(1)}, f32[2,256,256]{2,1,0:T(8,128)S(1)}, u32[]{:S(2)}, u32[]{:S(2)}) collective-permute-start(f32[2,256,256]{2,1,0:T(8,128)S(1)} %copy-done.10), channel_id=1, source_target_pairs={{0,16},{16,32},{32,48},{48,64},{64,80},{80,96},{96,112},{112,128},... | collective-permute-start | bytes 1572872 | tf_op jit(solution)/shard_map/ppermute | solution.py:24
  120.3 2.0 %collective-permute-start.23 = (f32[32,256]{1,0:T(8,128)S(1)}, f32[32,256]{1,0:T(8,128)S(1)}, u32[]{:S(2)}, u32[]{:S(2)}) collective-permute-start(f32[32,256]{1,0:T(8,128)S(1)} %get-tuple-element.15), channel_id=1, source_target_pairs={{0,192},{1,193},{32,224},{33,225},{64,0},{65,1},{96,32},{97,33},{1... | collective-permute-start | bytes 98312 | tf_op jit(solution)/shard_map/ppermute | solution.py:255
  122.3 3.4 %collective-permute-start.24 = (f32[32,256]{1,0:T(8,128)S(1)}, f32[32,256]{1,0:T(8,128)S(1)}, u32[]{:S(2)}, u32[]{:S(2)}) collective-permute-start(f32[32,256]{1,0:T(8,128)S(1)} %get-tuple-element.15), channel_id=1, source_target_pairs={{0,160},{1,161},{32,192},{33,193},{64,224},{65,225},{96,0},{97,1},... | collective-permute-start | bytes 98312 | tf_op jit(solution)/shard_map/ppermute | solution.py:255
  128.6 2.3 %collective-permute-start.26 = (f32[32,256]{1,0:T(8,128)S(1)}, f32[32,256]{1,0:T(8,128)S(1)}, u32[]{:S(2)}, u32[]{:S(2)}) collective-permute-start(f32[32,256]{1,0:T(8,128)S(1)} %get-tuple-element.15), channel_id=1, source_target_pairs={{0,96},{1,97},{32,128},{33,129},{64,160},{65,161},{96,192},{97,193... | collective-permute-start | bytes 98312 | tf_op jit(solution)/shard_map/ppermute | solution.py:255
  131.6 18.0 %collective-permute-done.25 = f32[32,256]{1,0:T(8,128)S(1)} collective-permute-done((f32[32,256]{1,0:T(8,128)S(1)}, f32[32,256]{1,0:T(8,128)S(1)}, u32[]{:S(2)}, u32[]{:S(2)}) %collective-permute-start.25) | collective-permute-done | bytes 32800 | tf_op jit(solution)/shard_map/ppermute | solution.py:255
  152.3 3.3 %collective-permute-done.27 = f32[32,256]{1,0:T(8,128)S(1)} collective-permute-done((f32[32,256]{1,0:T(8,128)S(1)}, f32[32,256]{1,0:T(8,128)S(1)}, u32[]{:S(2)}, u32[]{:S(2)}) %collective-permute-start.27) | collective-permute-done | bytes 32800 | tf_op jit(solution)/shard_map/ppermute | solution.py:255
  167.6 8.4 %collective-permute-done.6.above0_ref = f32[2,256,256]{2,1,0:T(8,128)S(1)} collective-permute-done((f32[2,256,256]{2,1,0:T(8,128)}, f32[2,256,256]{2,1,0:T(8,128)S(1)}, u32[]{:S(2)}, u32[]{:S(2)}) %collective-permute-start.6) | collective-permute-done | bytes 524320 | tf_op jit(solution)/shard_map/ppermute | solution.py:24
  176.8 4.2 %combined.1 = f32[2,512,512]{2,1,0:T(8,128)} custom-call(f32[2,512,512]{2,1,0:T(8,128)} %copy-done, f32[2,512,256]{2,1,0:T(8,128)} %collective-permute-done.4.left_ref, f32[2,256,256]{2,1,0:T(8,128)} %copy-done.18, f32[2,256,256]{2,1,0:T(8,128)} %copy-done.17), custom_call_target="tpu_custom_call" | custom-call | flops 1000000 | bytes 6291456 | tf_op jit(solution)/shard_map/combined/pallas_call | solution.py:224
  (102 shorter events, 49.2 us)
Async XLA Ops:
  3.1 32.6 %collective-permute-start = (f32[2,512,256]{2,1,0:T(8,128)}, f32[2,512,256]{2,1,0:T(8,128)S(1)}, u32[]{:S(2)}, u32[]{:S(2)}) collective-permute-start(f32[2,512,256]{2,1,0:T(8,128)} %slice.9), channel_id=1, source_target_pairs={{1,0},{2,1},{3,2},{4,3},{5,4},{6,5},{7,6},{8,7},{9,8},{10,9},{11,1... | collective-permute-start | bytes 3145736 | tf_op jit(solution)/shard_map/ppermute | solution.py:24
  5.4 19.0 %collective-permute-start.1 = (f32[2,256,256]{2,1,0:T(8,128)S(1)}, f32[2,256,256]{2,1,0:T(8,128)}, u32[]{:S(2)}, u32[]{:S(2)}) collective-permute-start(f32[2,256,256]{2,1,0:T(8,128)S(1)} %get-tuple-element.17), channel_id=1, source_target_pairs={{16,0},{32,16},{48,32},{64,48},{80,64},{96,80},{112,96},{128,112},... | collective-permute-start | bytes 1572872 | tf_op jit(solution)/shard_map/ppermute | solution.py:24
  9.4 26.3 %collective-permute-start.2 = (f32[2,256,256]{2,1,0:T(8,128)}, f32[2,256,256]{2,1,0:T(8,128)}, u32[]{:S(2)}, u32[]{:S(2)}) collective-permute-start(f32[2,256,256]{2,1,0:T(8,128)} %get-tuple-element.16), channel_id=1, source_target_pairs={{16,0},{32,16},{48,32},{64,48},{80,64},{96,80},{112,96},{128,112},... | collective-permute-start | bytes 1572872 | tf_op jit(solution)/shard_map/ppermute | solution.py:24
  24.4 12.2 %collective-permute-start.3 = (f32[2,256,256]{2,1,0:T(8,128)}, f32[2,256,256]{2,1,0:T(8,128)}, u32[]{:S(2)}, u32[]{:S(2)}) collective-permute-start(f32[2,256,256]{2,1,0:T(8,128)} %collective-permute-done.1.below0_hbm), channel_id=1, source_target_pairs={{1,0},{2,1},{3,2},{4,3},{5,4},{6,5},{7,6},{8,7},{9,8},{10,9},{11,1... | collective-permute-start | bytes 1572872 | tf_op jit(solution)/shard_map/ppermute | solution.py:24
  57.5 12.9 %collective-permute-start.15 = (f32[32,256]{1,0:T(8,128)S(1)}, f32[32,256]{1,0:T(8,128)S(1)}, u32[]{:S(2)}, u32[]{:S(2)}) collective-permute-start(f32[32,256]{1,0:T(8,128)S(1)} %get-tuple-element.19), channel_id=1, source_target_pairs={{0,224},{1,225},{32,0},{33,1},{64,32},{65,33},{96,64},{97,65},{128... | collective-permute-start | bytes 98312 | tf_op jit(solution)/shard_map/ppermute | solution.py:255
  58.9 15.2 %collective-permute-start.14 = (f32[32,256]{1,0:T(8,128)S(1)}, f32[32,256]{1,0:T(8,128)S(1)}, u32[]{:S(2)}, u32[]{:S(2)}) collective-permute-start(f32[32,256]{1,0:T(8,128)S(1)} %get-tuple-element.20), channel_id=1, source_target_pairs={{0,192},{1,193},{32,224},{33,225},{64,0},{65,1},{96,32},{97,33},{1... | collective-permute-start | bytes 98312 | tf_op jit(solution)/shard_map/ppermute | solution.py:255
  64.9 9.9 %collective-permute-start.13 = (f32[32,256]{1,0:T(8,128)S(1)}, f32[32,256]{1,0:T(8,128)S(1)}, u32[]{:S(2)}, u32[]{:S(2)}) collective-permute-start(f32[32,256]{1,0:T(8,128)S(1)} %get-tuple-element.21), channel_id=1, source_target_pairs={{0,160},{1,161},{32,192},{33,193},{64,224},{65,225},{96,0},{97,1},... | collective-permute-start | bytes 98312 | tf_op jit(solution)/shard_map/ppermute | solution.py:255
  66.2 8.6 %collective-permute-start.12 = (f32[32,256]{1,0:T(8,128)S(1)}, f32[32,256]{1,0:T(8,128)S(1)}, u32[]{:S(2)}, u32[]{:S(2)}) collective-permute-start(f32[32,256]{1,0:T(8,128)S(1)} %get-tuple-element.22), channel_id=1, source_target_pairs={{0,128},{1,129},{32,160},{33,161},{64,192},{65,193},{96,224},{97,2... | collective-permute-start | bytes 98312 | tf_op jit(solution)/shard_map/ppermute | solution.py:255
  70.4 7.4 %collective-permute-start.11 = (f32[32,256]{1,0:T(8,128)S(1)}, f32[32,256]{1,0:T(8,128)S(1)}, u32[]{:S(2)}, u32[]{:S(2)}) collective-permute-start(f32[32,256]{1,0:T(8,128)S(1)} %get-tuple-element.23), channel_id=1, source_target_pairs={{0,96},{1,97},{32,128},{33,129},{64,160},{65,161},{96,192},{97,193... | collective-permute-start | bytes 98312 | tf_op jit(solution)/shard_map/ppermute | solution.py:255
  70.4 7.4 %collective-permute-start.10 = (f32[32,256]{1,0:T(8,128)S(1)}, f32[32,256]{1,0:T(8,128)S(1)}, u32[]{:S(2)}, u32[]{:S(2)}) collective-permute-start(f32[32,256]{1,0:T(8,128)S(1)} %get-tuple-element.24), channel_id=1, source_target_pairs={{0,64},{1,65},{32,96},{33,97},{64,128},{65,129},{96,160},{97,161},... | collective-permute-start | bytes 98312 | tf_op jit(solution)/shard_map/ppermute | solution.py:255
  79.2 9.2 %collective-permute-start.18 = (f32[32,256]{1,0:T(8,128)S(1)}, f32[32,256]{1,0:T(8,128)S(1)}, u32[]{:S(2)}, u32[]{:S(2)}) collective-permute-start(f32[32,256]{1,0:T(8,128)S(1)} %add_add_fusion.2), channel_id=1, source_target_pairs={{0,6},{1,7},{32,38},{33,39},{64,70},{65,71},{96,102},{97,103},{128... | collective-permute-start | bytes 98312 | tf_op jit(solution)/shard_map/ppermute | solution.py:255
  86.8 5.5 %collective-permute-start.17 = (f32[32,256]{1,0:T(8,128)S(1)}, f32[32,256]{1,0:T(8,128)S(1)}, u32[]{:S(2)}, u32[]{:S(2)}) collective-permute-start(f32[32,256]{1,0:T(8,128)S(1)} %add_add_fusion.2), channel_id=1, source_target_pairs={{0,4},{1,5},{32,36},{33,37},{64,68},{65,69},{96,100},{97,101},{128... | collective-permute-start | bytes 98312 | tf_op jit(solution)/shard_map/ppermute | solution.py:255
  86.8 5.5 %collective-permute-start.16 = (f32[32,256]{1,0:T(8,128)S(1)}, f32[32,256]{1,0:T(8,128)S(1)}, u32[]{:S(2)}, u32[]{:S(2)}) collective-permute-start(f32[32,256]{1,0:T(8,128)S(1)} %add_add_fusion.2), channel_id=1, source_target_pairs={{0,2},{1,3},{32,34},{33,35},{64,66},{65,67},{96,98},{97,99},{128,1... | collective-permute-start | bytes 98312 | tf_op jit(solution)/shard_map/ppermute | solution.py:255
  92.3 13.4 %collective-permute-start.21 = (f32[32,256]{1,0:T(8,128)S(1)}, f32[32,256]{1,0:T(8,128)S(1)}, u32[]{:S(2)}, u32[]{:S(2)}) collective-permute-start(f32[32,256]{1,0:T(8,128)S(1)} %add_add_fusion.1), channel_id=1, source_target_pairs={{0,24},{1,25},{32,56},{33,57},{64,88},{65,89},{96,120},{97,121},{1... | collective-permute-start | bytes 98312 | tf_op jit(solution)/shard_map/ppermute | solution.py:255
  109.6 12.8 %collective-permute-start.22 = (f32[32,256]{1,0:T(8,128)S(1)}, f32[32,256]{1,0:T(8,128)S(1)}, u32[]{:S(2)}, u32[]{:S(2)}) collective-permute-start(f32[32,256]{1,0:T(8,128)S(1)} %get-tuple-element.15), channel_id=1, source_target_pairs={{0,224},{1,225},{32,0},{33,1},{64,32},{65,33},{96,64},{97,65},{128... | collective-permute-start | bytes 98312 | tf_op jit(solution)/shard_map/ppermute | solution.py:255
  110.0 57.6 %collective-permute-start.4 = (f32[2,512,256]{2,1,0:T(8,128)S(1)}, f32[2,512,256]{2,1,0:T(8,128)}, u32[]{:S(2)}, u32[]{:S(2)}) collective-permute-start(f32[2,512,256]{2,1,0:T(8,128)S(1)} %copy-done.5), channel_id=1, source_target_pairs={{0,1},{1,2},{2,3},{3,4},{4,5},{5,6},{6,7},{7,8},{8,9},{9,10},{10,1... | collective-permute-start | bytes 3145736 | tf_op jit(solution)/shard_map/ppermute | solution.py:24
  112.3 48.2 %collective-permute-start.5 = (f32[2,256,256]{2,1,0:T(8,128)S(1)}, f32[2,256,256]{2,1,0:T(8,128)S(1)}, u32[]{:S(2)}, u32[]{:S(2)}) collective-permute-start(f32[2,256,256]{2,1,0:T(8,128)S(1)} %copy-done.12), channel_id=1, source_target_pairs={{0,1},{1,2},{2,3},{3,4},{4,5},{5,6},{6,7},{7,8},{8,9},{9,10},{10,1... | collective-permute-start | bytes 1572872 | tf_op jit(solution)/shard_map/ppermute | solution.py:24
  114.1 53.5 %collective-permute-start.7 = (f32[2,256,256]{2,1,0:T(8,128)S(1)}, f32[2,256,256]{2,1,0:T(8,128)S(1)}, u32[]{:S(2)}, u32[]{:S(2)}) collective-permute-start(f32[2,256,256]{2,1,0:T(8,128)S(1)} %copy-done.10), channel_id=1, source_target_pairs={{0,16},{16,32},{32,48},{48,64},{64,80},{80,96},{96,112},{112,128},... | collective-permute-start | bytes 1572872 | tf_op jit(solution)/shard_map/ppermute | solution.py:24
  120.3 6.1 %collective-permute-start.23 = (f32[32,256]{1,0:T(8,128)S(1)}, f32[32,256]{1,0:T(8,128)S(1)}, u32[]{:S(2)}, u32[]{:S(2)}) collective-permute-start(f32[32,256]{1,0:T(8,128)S(1)} %get-tuple-element.15), channel_id=1, source_target_pairs={{0,192},{1,193},{32,224},{33,225},{64,0},{65,1},{96,32},{97,33},{1... | collective-permute-start | bytes 98312 | tf_op jit(solution)/shard_map/ppermute | solution.py:255
  122.3 6.3 %collective-permute-start.24 = (f32[32,256]{1,0:T(8,128)S(1)}, f32[32,256]{1,0:T(8,128)S(1)}, u32[]{:S(2)}, u32[]{:S(2)}) collective-permute-start(f32[32,256]{1,0:T(8,128)S(1)} %get-tuple-element.15), channel_id=1, source_target_pairs={{0,160},{1,161},{32,192},{33,193},{64,224},{65,225},{96,0},{97,1},... | collective-permute-start | bytes 98312 | tf_op jit(solution)/shard_map/ppermute | solution.py:255
  126.4 23.2 %collective-permute-start.25 = (f32[32,256]{1,0:T(8,128)S(1)}, f32[32,256]{1,0:T(8,128)S(1)}, u32[]{:S(2)}, u32[]{:S(2)}) collective-permute-start(f32[32,256]{1,0:T(8,128)S(1)} %get-tuple-element.15), channel_id=1, source_target_pairs={{0,128},{1,129},{32,160},{33,161},{64,192},{65,193},{96,224},{97,2... | collective-permute-start | bytes 98312 | tf_op jit(solution)/shard_map/ppermute | solution.py:255
  128.6 22.4 %collective-permute-start.26 = (f32[32,256]{1,0:T(8,128)S(1)}, f32[32,256]{1,0:T(8,128)S(1)}, u32[]{:S(2)}, u32[]{:S(2)}) collective-permute-start(f32[32,256]{1,0:T(8,128)S(1)} %get-tuple-element.15), channel_id=1, source_target_pairs={{0,96},{1,97},{32,128},{33,129},{64,160},{65,161},{96,192},{97,193... | collective-permute-start | bytes 98312 | tf_op jit(solution)/shard_map/ppermute | solution.py:255
  149.6 6.0 %collective-permute-start.27 = (f32[32,256]{1,0:T(8,128)S(1)}, f32[32,256]{1,0:T(8,128)S(1)}, u32[]{:S(2)}, u32[]{:S(2)}) collective-permute-start(f32[32,256]{1,0:T(8,128)S(1)} %get-tuple-element.15), channel_id=1, source_target_pairs={{0,64},{1,65},{32,96},{33,97},{64,128},{65,129},{96,160},{97,161},... | collective-permute-start | bytes 98312 | tf_op jit(solution)/shard_map/ppermute | solution.py:255
  161.4 14.6 %collective-permute-start.6 = (f32[2,256,256]{2,1,0:T(8,128)}, f32[2,256,256]{2,1,0:T(8,128)S(1)}, u32[]{:S(2)}, u32[]{:S(2)}) collective-permute-start(f32[2,256,256]{2,1,0:T(8,128)} %add.146), channel_id=1, source_target_pairs={{0,16},{16,32},{32,48},{48,64},{64,80},{80,96},{96,112},{112,128},... | collective-permute-start | bytes 1572872 | tf_op jit(solution)/shard_map/ppermute | solution.py:24
  (25 other events, 255.8 us)

commit v2 on v1

v2 whole, which is shorter than its diff:
```python
import functools
import math

import jax
import jax.numpy as jnp
import ml_dtypes
import numpy as np
from jax import lax
from jax.experimental import pallas as pl
from jax.experimental.pallas import tpu as pltpu
from jax.sharding import PartitionSpec as P

AXES = ("row", "col")
HBM = pl.BlockSpec(memory_space=pltpu.HBM)
SMEM = pl.BlockSpec(memory_space=pltpu.SMEM)
MIB = 1024 * 1024
SIZES = {"x": 4, "y": 4, "z": 8, "core": 2}


def shifted(block, axis, distance):
    devices = range(lax.axis_size(axis))
    route = [(i - distance, i) for i in devices if i - distance in devices]
    return lax.ppermute(block, axis, route)


def dft_tables(window):
    index = np.arange(window)
    phases = (np.outer(index, index) % window) * (2.0 * math.pi / window)
    tables = []
    for part in (np.cos(phases), -np.sin(phases)):
        part = part / math.sqrt(window)
        high = part.astype(ml_dtypes.bfloat16)
        tables += [high, (part - high.astype(np.float64)).astype(ml_dtypes.bfloat16)]
    return np.stack(tables)


def split(value):
    high = value.astype(jnp.bfloat16)
    return high, (value - high.astype(jnp.float32)).astype(jnp.bfloat16)


def dot(first, second):
    return jnp.dot(first, second, preferred_element_type=jnp.float32)


def times_table(re, im, tables, sign):
    w = re.shape[0]
    high, low = split(jnp.concatenate([re, im], axis=0))
    by_re = dot(high, tables[0]) + (dot(low, tables[0]) + dot(high, tables[1]))
    by_im = dot(high, tables[2]) + (dot(low, tables[2]) + dot(high, tables[3]))
    if sign > 0:
        return by_re[:w] - by_im[w:], by_re[w:] + by_im[:w]
    return by_re[:w] + by_im[w:], by_re[w:] - by_im[:w]


def table_times(re, im, tables, sign):
    w = re.shape[1]
    high, low = split(jnp.concatenate([re, im], axis=1))
    by_re = dot(tables[0], high) + (dot(tables[0], low) + dot(tables[1], high))
    by_im = dot(tables[2], high) + (dot(tables[2], low) + dot(tables[3], high))
    if sign > 0:
        return by_re[:, :w] - by_im[:, w:], by_re[:, w:] + by_im[:, :w]
    return by_re[:, :w] + by_im[:, w:], by_re[:, w:] - by_im[:, :w]


def slots_kernel(
    window, tile,
    counts_ref, pos_ref, place_ref, object_hbm, right0_hbm, right1_hbm, relayed_hbm, below0_hbm, below1_hbm,
    corner_hbm, diagonal_hbm, probe_hbm, amp_hbm, tables_hbm,
    tile_out, right_out, below0_out, below1_out, corner_out, keep_out, send_out,
    ext, grad, probe, turned, amp, tables, patch, probe_grad, sems,
):
    w, t = window, tile
    e = t + w
    live = counts_ref[0]
    core, at_seam = place_ref[0], place_ref[1]
    moves = [
        (probe_hbm, probe),
        (tables_hbm, tables),
        (amp_hbm, amp),
        (object_hbm, ext.at[:, 0:t, 0:t]),
        (right0_hbm, ext.at[:, 0:w, t:e]),
        (below0_hbm, ext.at[:, t:e, 0:w]),
        (below1_hbm, ext.at[:, t:e, w:t]),
    ]
    copies = [pltpu.make_async_copy(a, b, sems.at[i]) for i, (a, b) in enumerate(moves)]
    for copy in copies:
        copy.start()

    def choose(act):
        for flag, lower, last in ((0, right1_hbm, corner_hbm), (1, relayed_hbm, diagonal_hbm)):
            @pl.when(at_seam == flag)
            def _():
                act(pltpu.make_async_copy(lower, ext.at[:, w:t, t:e], sems.at[7]))
                act(pltpu.make_async_copy(last, ext.at[:, t:e, t:e], sems.at[8]))

    choose(lambda copy: copy.start())
    grad[...] = jnp.zeros_like(grad)
    probe_grad[...] = jnp.zeros_like(probe_grad)
    copies[0].wait()

    def turn(slot, carry):
        row = lax.rem(lax.rem(pos_ref[slot, 0], t), w)
        col = lax.rem(lax.rem(pos_ref[slot, 1], t), w)
        for plane in range(2):
            turned[slot, plane] = pltpu.roll(pltpu.roll(probe[plane], row, 0), col, 1)
        return carry

    lax.fori_loop(0, live, turn, 0)
    for copy in copies[1:]:
        copy.wait()
    choose(lambda copy: copy.wait())
    moves = [
        (grad.at[:, t:e, t:e], corner_out),
        (grad.at[:, t:e, w:t], below1_out),
        (grad.at[:, t:e, 0:w], below0_out),
        (grad.at[:, 0:t, t:e], right_out),
        (grad.at[:, 0:t, 0:t], tile_out),
    ]
    results = [pltpu.make_async_copy(a, b, sems.at[i]) for i, (a, b) in enumerate(moves)]
    rows = lax.broadcasted_iota(jnp.int32, (w, w), 0)
    cols = lax.broadcasted_iota(jnp.int32, (w, w), 1)

    def one_slot(slot, carry):
        top = lax.rem(pos_ref[slot, 0], t)
        left = lax.rem(pos_ref[slot, 1], t)
        row_turn, col_turn = lax.rem(top, w), lax.rem(left, w)
        row_at = pl.multiple_of((top // w) * w, w)
        col_at = pl.multiple_of((left // w) * w, w)
        in_low = rows < row_turn
        in_right = cols < col_turn
        blocks = [
            (pl.ds(row_at, w), pl.ds(col_at, w), ~in_low & ~in_right),
            (pl.ds(row_at, w), pl.ds(col_at + w, w), ~in_low & in_right),
            (pl.ds(row_at + w, w), pl.ds(col_at, w), in_low & ~in_right),
            (pl.ds(row_at + w, w), pl.ds(col_at + w, w), in_low & in_right),
        ]
        for plane in range(2):
            parts = [ext[plane, at_rows, at_cols] for at_rows, at_cols, _ in blocks]
            patch[plane] = jnp.where(
                in_low, jnp.where(in_right, parts[3], parts[2]), jnp.where(in_right, parts[1], parts[0])
            )
        re = turned[slot, 0] * patch[0] - turned[slot, 1] * patch[1]
        im = turned[slot, 0] * patch[1] + turned[slot, 1] * patch[0]
        re, im = times_table(re, im, tables, 1)
        re, im = table_times(re, im, tables, 1)
        factor = 1.0 - amp[slot] / jnp.sqrt(re * re + im * im + 1.0)
        re, im = times_table(factor * re, factor * im, tables, -1)
        re, im = table_times(re, im, tables, -1)
        terms = (turned[slot, 0] * re + turned[slot, 1] * im, turned[slot, 0] * im - turned[slot, 1] * re)
        for at_rows, at_cols, mask in blocks:
            for plane in range(2):
                grad[plane, at_rows, at_cols] += jnp.where(mask, terms[plane], 0.0)

        @pl.when(slot == live - 1)
        def _():
            for copy in results:
                copy.start()

        terms = (patch[0] * re + patch[1] * im, patch[0] * im - patch[1] * re)
        for plane in range(2):
            term = pltpu.roll(terms[plane], lax.rem(w - row_turn, w), 0)
            probe_grad[plane] += pltpu.roll(term, lax.rem(w - col_turn, w), 1)
        return carry

    lax.fori_loop(0, live, one_slot, 0)
    keep = pltpu.make_async_copy(probe_grad.at[core], keep_out, sems.at[7])
    send = pltpu.make_async_copy(probe_grad.at[1 - core], send_out, sems.at[8])
    for copy in (send, keep):
        copy.start()
    for copy in (send, keep, *results):
        copy.wait()


def slot_terms(counts, positions, where, object_field, halos, probe, amplitudes):
    w, t = probe.shape[1], object_field.shape[1]
    slots = positions.shape[0]
    f32 = functools.partial(jax.ShapeDtypeStruct, dtype=jnp.float32)
    block = f32((2, w, w))
    return pl.pallas_call(
        functools.partial(slots_kernel, w, t),
        out_shape=[f32((2, t, t)), f32((2, t, w)), block, block, block, f32((w, w)), f32((w, w))],
        in_specs=[SMEM] * 3 + [HBM] * 11,
        out_specs=[HBM] * 7,
        scratch_shapes=[
            pltpu.VMEM((2, t + w, t + w), jnp.float32),
            pltpu.VMEM((2, t + w, t + w), jnp.float32),
            pltpu.VMEM((2, w, w), jnp.float32),
            pltpu.VMEM((slots, 2, w, w), jnp.float32),
            pltpu.VMEM((slots, w, w), jnp.float32),
            pltpu.VMEM((4, w, w), jnp.bfloat16),
            pltpu.VMEM((2, w, w), jnp.float32),
            pltpu.VMEM((2, w, w), jnp.float32),
            pltpu.SemaphoreType.DMA((9,)),
        ],
        compiler_params=pltpu.CompilerParams(vmem_limit_bytes=60 * MIB),
        cost_estimate=pl.CostEstimate(flops=3 * 10**9, bytes_accessed=14 * MIB, transcendentals=0),
        name="slot_terms",
    )(counts, positions, where, object_field, *halos, probe, amplitudes, jnp.asarray(dft_tables(w)))


def combine_kernel(half, tile_ref, left_ref, above0_ref, above1_ref, out_ref):
    w = left_ref.shape[2]
    first, second = tile_ref[:, :, :w] + left_ref[...], tile_ref[:, :, w:]

    @pl.when(pl.program_id(0) < half)
    def _():
        out_ref[:, :, :w] = first + above0_ref[...]
        out_ref[:, :, w:] = second + above1_ref[...]

    @pl.when(pl.program_id(0) >= half)
    def _():
        out_ref[:, :, :w] = first
        out_ref[:, :, w:] = second


def combined(tile_grad, from_left, above0, above1):
    t, w = tile_grad.shape[1], from_left.shape[2]
    step = w // 2
    half = w // step
    above = pl.BlockSpec((2, step, w), lambda i: (0, jnp.minimum(i, half - 1), 0))
    return pl.pallas_call(
        functools.partial(combine_kernel, half),
        out_shape=jax.ShapeDtypeStruct(tile_grad.shape, jnp.float32),
        grid=(t // step,),
        in_specs=[
            pl.BlockSpec((2, step, t), lambda i: (0, i, 0)),
            pl.BlockSpec((2, step, w), lambda i: (0, i, 0)),
            above,
            above,
        ],
        out_specs=pl.BlockSpec((2, step, t), lambda i: (0, i, 0)),
        cost_estimate=pl.CostEstimate(flops=10**6, bytes_accessed=6 * MIB, transcendentals=0),
        name="combined",
    )(tile_grad, from_left, above0, above1)


def place(x, y, z, core):
    return (z % 8 * 2 + y % 4 // 2) * 16 + y % 2 * 8 + x % 4 * 2 + core % 2


def moved(value, **distance):
    route = []
    for x in range(4):
        for y in range(4):
            for z in range(8):
                for core in range(2):
                    target = place(
                        x + distance.get("x", 0), y + distance.get("y", 0),
                        z + distance.get("z", 0), core + distance.get("core", 0),
                    )
                    route.append((place(x, y, z, core), target))
    return lax.ppermute(value, AXES, route)


def summed(value, axis):
    parts = [moved(value, **{axis: d}) for d in range(1, SIZES[axis])]
    return functools.reduce(jnp.add, parts, value)


def z_exchange(chunks):
    groups = [[place(x, y, z, c) for z in range(8)] for x in range(4) for y in range(4) for c in range(2)]
    return lax.all_to_all(chunks, AXES, 0, 0, tiled=True, axis_index_groups=groups)


def total(keep, send, core):
    if (lax.axis_size("row"), lax.axis_size("col")) != (16, 16):
        return lax.psum(jnp.where(core == 0, jnp.stack([keep, send]), jnp.stack([send, keep])), AXES)
    w = keep.shape[0]
    value = keep + moved(send, core=1)
    value = jnp.sum(z_exchange(value.reshape(8, w // 8, w)), axis=0)
    value = summed(summed(value, "x"), "y")
    value = z_exchange(jnp.broadcast_to(value, (8,) + value.shape)).reshape(w, w)
    other = moved(value, core=1)
    return jnp.where(core == 0, jnp.stack([value, other]), jnp.stack([other, value]))


def halos_in(object_field, window):
    rows, cols = lax.axis_size("row"), lax.axis_size("col")
    seam = cols // 2
    w = window
    below0_own = object_field[:, :w, :w]
    right1_own = object_field[:, w:, :w]
    below0 = shifted(below0_own, "row", -1)
    below1 = shifted(object_field[:, :w, w:], "row", -1)
    relayed = lax.ppermute(right1_own, "col", [(seam, 0)])
    right0 = shifted(below0_own, "col", -1)
    plain = [(i + 1, i) for i in range(cols - 1) if i + 1 != seam]
    right1 = lax.ppermute(right1_own, "col", plain)
    route = [((r + 1) * cols + seam, r * cols + seam - 1) for r in range(rows - 1)]
    diagonal = lax.ppermute(below0_own, AXES, route)
    relayed = lax.ppermute(relayed, "col", [(0, seam - 1)])
    corner = lax.ppermute(below0, "col", plain)
    return right0, right1, relayed, below0, below1, corner, diagonal


def shards(object_field, probe, positions, amplitudes, counts):
    window = probe.shape[1]
    col = lax.axis_index("col")
    core = col % 2
    at_seam = (col == lax.axis_size("col") // 2 - 1).astype(jnp.int32)
    halos = halos_in(object_field, window)
    where = jnp.stack([core, at_seam])
    tile_grad, right_grad, below0_grad, below1_grad, corner_grad, keep, send = slot_terms(
        counts, positions, where, object_field, halos, probe, amplitudes
    )
    corner_in = shifted(corner_grad, "col", 1)
    above1 = shifted(below1_grad, "row", 1)
    from_left = shifted(right_grad, "col", 1)
    above0 = shifted(below0_grad + corner_in, "row", 1)
    probe_total = total(keep, send, core)
    return combined(tile_grad, from_left, above0, above1), probe_total


def solution(mesh):
    return jax.shard_map(
        shards,
        mesh=mesh,
        in_specs=(
            P(None, "row", "col"),
            P(),
            P(("row", "col"), None),
            P(("row", "col"), None, None),
            P(("row", "col")),
        ),
        out_specs=(P(None, "row", "col"), P()),
        check_vma=False,
    )
```

time: 182 us -> 153 us (0.84)
  the two profiles are of different devices: /device:TPU:16 before, /device:TPU:32 now
where the time goes in v2:
time: 153 us
  waiting for transfers between devices  64.9 us (42%)
  starting transfers between devices  44.4 us (29%)
  blocking collectives  22.1 us (14%)
  Pallas kernels  14.4 us (9%)
  local copies, waits for them, and re-layouts  3.38 us (2%)
  other arithmetic  2.54 us (2%)
  between operations  1.53 us (1%)
    ppermute x7, waiting for transfers between devices, shifted(): return lax.ppermute(block, axis, route)  26.3 us
    ppermute x7, starting transfers between devices, shifted(): return lax.ppermute(block, axis, route)  24.2 us
    all_to_all x1, blocking collectives, z_exchange(): lax.all_to_all(chunks, AXES, 0, 0, tiled=True, axis_index_groups=groups)  22.1 us
    ppermute x8, waiting for transfers between devices, moved(): return lax.ppermute(value, AXES, route)  16.8 us
    ppermute x1, waiting for transfers between devices, halos_in(): relayed = lax.ppermute(right1_own, 'col', [(seam, 0)])  15.8 us
    pallas_call x1, Pallas kernels, slot_terms(): pl.pallas_call(functools.partial(slots_kernel, w, t), out_shape=[f32((2,...  10.2 us
    ppermute x8, starting transfers between devices, moved(): return lax.ppermute(value, AXES, route)  8.82 us
    all_to_all x1, starting transfers between devices, z_exchange(): lax.all_to_all(chunks, AXES, 0, 0, tiled=True, axis_index_groups=groups)  4.78 us
  transfers between devices with their start and end apart: 21, of which 9 were waited for; matrix products, arithmetic and copies ran while one was open for 1% of the time, Pallas kernels for 3%

profile of v2, /device:TPU:32, one launch (start us, length us, event | category | flops | bytes accessed | tf_op | source)
XLA Modules:
  0.0 153.2 jit_solution(9213101675738147845)
XLA Ops:
  0.6 1.5 fusion
  2.1 4.6 %collective-permute-start.5 = (f32[2,256,256]{2,1,0:T(8,128)S(1)}, f32[2,256,256]{2,1,0:T(8,128)S(1)}, u32[]{:S(2)}, u32[]{:S(2)}) collective-permute-start(f32[2,256,256]{2,1,0:T(8,128)S(1)} %get-tuple-element.16), channel_id=1, source_target_pairs={{16,0},{32,16},{48,32},{64,48},{80,64},{96,80},{112,96},{128,112},... | collective-permute-start | bytes 1572872 | tf_op jit(solution)/shard_map/ppermute | solution.py:23
  8.1 4.0 %collective-permute-start.4 = (f32[2,256,256]{2,1,0:T(8,128)S(1)}, f32[2,256,256]{2,1,0:T(8,128)S(1)}, u32[]{:S(2)}, u32[]{:S(2)}) collective-permute-start(f32[2,256,256]{2,1,0:T(8,128)S(1)} %get-tuple-element.18), channel_id=1, source_target_pairs={{16,0},{32,16},{48,32},{64,48},{80,64},{96,80},{112,96},{128,112},... | collective-permute-start | bytes 1572872 | tf_op jit(solution)/shard_map/ppermute | solution.py:23
  14.1 6.3 %collective-permute-done.5.below1_hbm = f32[2,256,256]{2,1,0:T(8,128)S(1)} collective-permute-done((f32[2,256,256]{2,1,0:T(8,128)S(1)}, f32[2,256,256]{2,1,0:T(8,128)S(1)}, u32[]{:S(2)}, u32[]{:S(2)}) %collective-permute-start.5) | collective-permute-done | bytes 524320 | tf_op jit(solution)/shard_map/ppermute | solution.py:23
  21.6 15.8 %collective-permute-done.2 = f32[2,256,256]{2,1,0:T(8,128)} collective-permute-done((f32[2,256,256]{2,1,0:T(8,128)S(1)}, f32[2,256,256]{2,1,0:T(8,128)}, u32[]{:S(2)}, u32[]{:S(2)}) %collective-permute-start.2) | collective-permute-done | bytes 524320 | tf_op jit(solution)/shard_map/ppermute | solution.py:286
  37.4 2.1 %collective-permute-start.3 = (f32[2,256,256]{2,1,0:T(8,128)}, f32[2,256,256]{2,1,0:T(8,128)}, u32[]{:S(2)}, u32[]{:S(2)}) collective-permute-start(f32[2,256,256]{2,1,0:T(8,128)} %collective-permute-done.2), channel_id=1, source_target_pairs={{0,7},{16,23},{32,39},{48,55},{64,71},{80,87},{96,103},{112,119},{... | collective-permute-start | bytes 1572872 | tf_op jit(solution)/shard_map/ppermute | solution.py:292
  42.1 3.6 %collective-permute-done.3.relayed_hbm = f32[2,256,256]{2,1,0:T(8,128)} collective-permute-done((f32[2,256,256]{2,1,0:T(8,128)}, f32[2,256,256]{2,1,0:T(8,128)}, u32[]{:S(2)}, u32[]{:S(2)}) %collective-permute-start.3) | collective-permute-done | bytes 524320 | tf_op jit(solution)/shard_map/ppermute | solution.py:292
  45.7 10.2 %slot_terms.1 = (f32[2,512,512]{2,1,0:T(8,128)}, f32[2,512,256]{2,1,0:T(8,128)}, f32[2,256,256]{2,1,0:T(8,128)}, f32[2,256,256]{2,1,0:T(8,128)}, f32[2,256,256]{...) custom-call(s32[1]{0:T(128)S(6)} %copy.8.counts_ref, s32[2,2]{1,0:T(2,128)} %pos_ref.1, s32[2]{0:T(128)} %pad_add_fusion.place_ref, ...), custom_call_target="tpu_custom_call" | custom-call | flops 3000000000 | bytes 14680064 | tf_op jit(solution)/shard_map/slot_terms/pallas_call | solution.py:180
  56.0 1.7 %collective-permute-done.12 = f32[256,256]{1,0:T(8,128)S(1)} collective-permute-done((f32[256,256]{1,0:T(8,128)}, f32[256,256]{1,0:T(8,128)S(1)}, u32[]{:S(2)}, u32[]{:S(2)}) %collective-permute-start.12) | collective-permute-done | bytes 262176 | tf_op jit(solution)/shard_map/ppermute | solution.py:253
  58.7 22.1 %all_to_all.10 = f32[8,32,256]{2,1,0:T(8,128)S(1)} all-to-all(f32[8,32,256]{2,1,0:T(8,128)S(1)} %bitcast.6), channel_id=1, replica_groups={{0,32,64,96,128,160,192,224},{1,33,65,97,129,161,193,225},{8,40,72,104,..., dimensions={0} | all-to-all | bytes 524288 | tf_op jit(solution)/shard_map/all_to_all | solution.py:263
  80.8 5.2 %collective-permute-start.15 = (f32[32,256]{1,0:T(8,128)S(1)}, f32[32,256]{1,0:T(8,128)S(1)}, u32[]{:S(2)}, u32[]{:S(2)}) collective-permute-start(f32[32,256]{1,0:T(8,128)S(1)} %reduce_sum.9), channel_id=1, source_target_pairs={{0,6},{1,7},{32,38},{33,39},{64,70},{65,71},{96,102},{97,103},{128... | collective-permute-start | bytes 98312 | tf_op jit(solution)/shard_map/ppermute | solution.py:253
  86.1 1.3 collective-permute-start.13
  87.5 1.3 collective-permute-start.9
  88.8 4.7 %collective-permute-start.8 = (f32[2,512,256]{2,1,0:T(8,128)}, f32[2,512,256]{2,1,0:T(8,128)S(1)}, u32[]{:S(2)}, u32[]{:S(2)}) collective-permute-start(f32[2,512,256]{2,1,0:T(8,128)} %get-tuple-element.10), channel_id=1, source_target_pairs={{0,1},{1,2},{2,3},{3,4},{4,5},{5,6},{6,7},{7,8},{8,9},{9,10},{10,1... | collective-permute-start | bytes 3145736 | tf_op jit(solution)/shard_map/ppermute | solution.py:23
  93.7 1.9 %collective-permute-start.16 = (f32[32,256]{1,0:T(8,128)S(1)}, f32[32,256]{1,0:T(8,128)S(1)}, u32[]{:S(2)}, u32[]{:S(2)}) collective-permute-start(f32[32,256]{1,0:T(8,128)S(1)} %add_add_fusion.1), channel_id=1, source_target_pairs={{0,8},{1,9},{32,40},{33,41},{64,72},{65,73},{96,104},{97,105},{128... | collective-permute-start | bytes 98312 | tf_op jit(solution)/shard_map/ppermute | solution.py:253
  95.6 1.9 %collective-permute-done.18 = f32[32,256]{1,0:T(8,128)S(1)} collective-permute-done((f32[32,256]{1,0:T(8,128)S(1)}, f32[32,256]{1,0:T(8,128)S(1)}, u32[]{:S(2)}, u32[]{:S(2)}) %collective-permute-start.18) | collective-permute-done | bytes 32800 | tf_op jit(solution)/shard_map/ppermute | solution.py:253
  97.5 13.2 %collective-permute-done.17 = f32[32,256]{1,0:T(8,128)S(1)} collective-permute-done((f32[32,256]{1,0:T(8,128)S(1)}, f32[32,256]{1,0:T(8,128)S(1)}, u32[]{:S(2)}, u32[]{:S(2)}) %collective-permute-start.17) | collective-permute-done | bytes 32800 | tf_op jit(solution)/shard_map/ppermute | solution.py:253
  111.4 4.8 %all-to-all-start.1 = ((f32[8,32,256]{2,1,0:T(8,128)}), f32[8,32,256]{2,1,0:T(8,128)S(1)}, u32[]{:S(2)}, u32[]{:S(2)}) async-start(f32[8,32,256]{2,1,0:T(8,128)} %broadcast_in_dim.3), calls=%async_computation.1 | async-start | bytes 524288 | tf_op jit(solution)/shard_map/all_to_all | solution.py:263
  116.2 3.5 %collective-permute-start.11 = (f32[2,256,256]{2,1,0:T(8,128)}, f32[2,256,256]{2,1,0:T(8,128)S(1)}, u32[]{:S(2)}, u32[]{:S(2)}) collective-permute-start(f32[2,256,256]{2,1,0:T(8,128)} %get-tuple-element.13), channel_id=1, source_target_pairs={{0,16},{16,32},{32,48},{48,64},{64,80},{80,96},{96,112},{112,128},... | collective-permute-start | bytes 1572872 | tf_op jit(solution)/shard_map/ppermute | solution.py:23
  119.8 4.7 %collective-permute-start.10 = (f32[2,256,256]{2,1,0:T(8,128)S(1)}, f32[2,256,256]{2,1,0:T(8,128)S(1)}, u32[]{:S(2)}, u32[]{:S(2)}) collective-permute-start(f32[2,256,256]{2,1,0:T(8,128)S(1)} %add.29), channel_id=1, source_target_pairs={{0,16},{16,32},{32,48},{48,64},{64,80},{80,96},{96,112},{112,128},... | collective-permute-start | bytes 1572872 | tf_op jit(solution)/shard_map/ppermute | solution.py:23
  124.6 2.5 %all-to-all-done.1 = f32[8,32,256]{2,1,0:T(8,128)S(1)} async-done(((f32[8,32,256]{2,1,0:T(8,128)}), f32[8,32,256]{2,1,0:T(8,128)S(1)}, u32[]{:S(2)}, u32[]{:S(2)}) %all-to-all-start.1) | async-done | bytes 262176 | tf_op jit(solution)/shard_map/all_to_all | solution.py:263
  127.0 9.0 %collective-permute-done.11.above1_ref = f32[2,256,256]{2,1,0:T(8,128)S(1)} collective-permute-done((f32[2,256,256]{2,1,0:T(8,128)}, f32[2,256,256]{2,1,0:T(8,128)S(1)}, u32[]{:S(2)}, u32[]{:S(2)}) %collective-permute-start.11) | collective-permute-done | bytes 524320 | tf_op jit(solution)/shard_map/ppermute | solution.py:23
  136.0 11.0 %collective-permute-done.10.above0_ref = f32[2,256,256]{2,1,0:T(8,128)S(1)} collective-permute-done((f32[2,256,256]{2,1,0:T(8,128)S(1)}, f32[2,256,256]{2,1,0:T(8,128)S(1)}, u32[]{:S(2)}, u32[]{:S(2)}) %collective-permute-start.10) | collective-permute-done | bytes 524320 | tf_op jit(solution)/shard_map/ppermute | solution.py:23
  148.2 4.2 %combined.1 = f32[2,512,512]{2,1,0:T(8,128)} custom-call(f32[2,512,512]{2,1,0:T(8,128)} %get-tuple-element.9.tile_ref, f32[2,512,256]{2,1,0:T(8,128)} %copy-done, f32[2,256,256]{2,1,0:T(8,128)} %copy-done.3, f32[2,256,256]{2,1,0:T(8,128)} %copy-done.2), custom_call_target="tpu_custom_call" | custom-call | flops 1000000 | bytes 6291456 | tf_op jit(solution)/shard_map/combined/pallas_call | solution.py:222
  (46 shorter events, 10.7 us)
Async XLA Ops:
  2.1 18.2 %collective-permute-start.5 = (f32[2,256,256]{2,1,0:T(8,128)S(1)}, f32[2,256,256]{2,1,0:T(8,128)S(1)}, u32[]{:S(2)}, u32[]{:S(2)}) collective-permute-start(f32[2,256,256]{2,1,0:T(8,128)S(1)} %get-tuple-element.16), channel_id=1, source_target_pairs={{16,0},{32,16},{48,32},{64,48},{80,64},{96,80},{112,96},{128,112},... | collective-permute-start | bytes 1572872 | tf_op jit(solution)/shard_map/ppermute | solution.py:23
  6.8 30.6 %collective-permute-start.2 = (f32[2,256,256]{2,1,0:T(8,128)S(1)}, f32[2,256,256]{2,1,0:T(8,128)}, u32[]{:S(2)}, u32[]{:S(2)}) collective-permute-start(f32[2,256,256]{2,1,0:T(8,128)S(1)} %get-tuple-element.17), channel_id=1, source_target_pairs={{8,0},{24,16},{40,32},{56,48},{72,64},{88,80},{104,96},{120,112},{... | collective-permute-start | bytes 1572872 | tf_op jit(solution)/shard_map/ppermute | solution.py:286
  8.1 31.4 %collective-permute-start.4 = (f32[2,256,256]{2,1,0:T(8,128)S(1)}, f32[2,256,256]{2,1,0:T(8,128)S(1)}, u32[]{:S(2)}, u32[]{:S(2)}) collective-permute-start(f32[2,256,256]{2,1,0:T(8,128)S(1)} %get-tuple-element.18), channel_id=1, source_target_pairs={{16,0},{32,16},{48,32},{64,48},{80,64},{96,80},{112,96},{128,112},... | collective-permute-start | bytes 1572872 | tf_op jit(solution)/shard_map/ppermute | solution.py:23
  12.1 30.0 %collective-permute-start.1 = (f32[2,256,256]{2,1,0:T(8,128)S(1)}, f32[2,256,256]{2,1,0:T(8,128)S(1)}, u32[]{:S(2)}, u32[]{:S(2)}) collective-permute-start(f32[2,256,256]{2,1,0:T(8,128)S(1)} %get-tuple-element.17), channel_id=1, source_target_pairs={{1,0},{2,1},{3,2},{4,3},{5,4},{6,5},{7,6},{9,8},{10,9},{11,10},{12... | collective-permute-start | bytes 1572872 | tf_op jit(solution)/shard_map/ppermute | solution.py:289
  13.4 28.7 %collective-permute-start.7 = (f32[2,256,256]{2,1,0:T(8,128)S(1)}, f32[2,256,256]{2,1,0:T(8,128)S(1)}, u32[]{:S(2)}, u32[]{:S(2)}) collective-permute-start(f32[2,256,256]{2,1,0:T(8,128)S(1)} %get-tuple-element.18), channel_id=1, source_target_pairs={{24,7},{40,23},{56,39},{72,55},{88,71},{104,87},{120,103},{136,119... | collective-permute-start | bytes 1572872 | tf_op jit(solution)/shard_map/ppermute | solution.py:291
  20.3 25.3 %copy-start.4 = (f32[2,256,256]{2,1,0:T(8,128)}, f32[2,256,256]{2,1,0:T(8,128)S(1)}, u32[]{:S(2)}) copy-start(f32[2,256,256]{2,1,0:T(8,128)S(1)} %collective-permute-done.5.below1_hbm) | copy-start | bytes 1572868
  20.3 21.7 %collective-permute-start = (f32[2,256,256]{2,1,0:T(8,128)S(1)}, f32[2,256,256]{2,1,0:T(8,128)}, u32[]{:S(2)}, u32[]{:S(2)}) collective-permute-start(f32[2,256,256]{2,1,0:T(8,128)S(1)} %get-tuple-element.18), channel_id=1, source_target_pairs={{1,0},{2,1},{3,2},{4,3},{5,4},{6,5},{7,6},{8,7},{9,8},{10,9},{11,1... | collective-permute-start | bytes 1572872 | tf_op jit(solution)/shard_map/ppermute | solution.py:23
  37.4 8.3 %collective-permute-start.3 = (f32[2,256,256]{2,1,0:T(8,128)}, f32[2,256,256]{2,1,0:T(8,128)}, u32[]{:S(2)}, u32[]{:S(2)}) collective-permute-start(f32[2,256,256]{2,1,0:T(8,128)} %collective-permute-done.2), channel_id=1, source_target_pairs={{0,7},{16,23},{32,39},{48,55},{64,71},{80,87},{96,103},{112,119},{... | collective-permute-start | bytes 1572872 | tf_op jit(solution)/shard_map/ppermute | solution.py:292
  39.5 6.2 %collective-permute-start.6 = (f32[2,256,256]{2,1,0:T(8,128)S(1)}, f32[2,256,256]{2,1,0:T(8,128)}, u32[]{:S(2)}, u32[]{:S(2)}) collective-permute-start(f32[2,256,256]{2,1,0:T(8,128)S(1)} %collective-permute-done.4.below0_hbm), channel_id=1, source_target_pairs={{1,0},{2,1},{3,2},{4,3},{5,4},{6,5},{7,6},{9,8},{10,9},{11,10},{12... | collective-permute-start | bytes 1572872 | tf_op jit(solution)/shard_map/ppermute | solution.py:293
  55.9 63.8 %copy-start.1 = (f32[2,256,256]{2,1,0:T(8,128)S(1)}, f32[2,256,256]{2,1,0:T(8,128)}, u32[]{:S(2)}) copy-start(f32[2,256,256]{2,1,0:T(8,128)} %get-tuple-element.11) | copy-start | bytes 1572868
  55.9 1.8 %collective-permute-start.12 = (f32[256,256]{1,0:T(8,128)}, f32[256,256]{1,0:T(8,128)S(1)}, u32[]{:S(2)}, u32[]{:S(2)}) collective-permute-start(f32[256,256]{1,0:T(8,128)} %get-tuple-element.15), channel_id=1, source_target_pairs={{0,1},{1,0},{32,33},{33,32},{64,65},{65,64},{96,97},{97,96},{128,1... | collective-permute-start | bytes 786440 | tf_op jit(solution)/shard_map/ppermute | solution.py:253
  80.8 12.7 %collective-permute-start.15 = (f32[32,256]{1,0:T(8,128)S(1)}, f32[32,256]{1,0:T(8,128)S(1)}, u32[]{:S(2)}, u32[]{:S(2)}) collective-permute-start(f32[32,256]{1,0:T(8,128)S(1)} %reduce_sum.9), channel_id=1, source_target_pairs={{0,6},{1,7},{32,38},{33,39},{64,70},{65,71},{96,102},{97,103},{128... | collective-permute-start | bytes 98312 | tf_op jit(solution)/shard_map/ppermute | solution.py:253
  86.0 7.5 %collective-permute-start.14 = (f32[32,256]{1,0:T(8,128)S(1)}, f32[32,256]{1,0:T(8,128)S(1)}, u32[]{:S(2)}, u32[]{:S(2)}) collective-permute-start(f32[32,256]{1,0:T(8,128)S(1)} %reduce_sum.9), channel_id=1, source_target_pairs={{0,4},{1,5},{32,36},{33,37},{64,68},{65,69},{96,100},{97,101},{128... | collective-permute-start | bytes 98312 | tf_op jit(solution)/shard_map/ppermute | solution.py:253
  86.1 7.4 %collective-permute-start.13 = (f32[32,256]{1,0:T(8,128)S(1)}, f32[32,256]{1,0:T(8,128)S(1)}, u32[]{:S(2)}, u32[]{:S(2)}) collective-permute-start(f32[32,256]{1,0:T(8,128)S(1)} %reduce_sum.9), channel_id=1, source_target_pairs={{0,2},{1,3},{32,34},{33,35},{64,66},{65,67},{96,98},{97,99},{128,1... | collective-permute-start | bytes 98312 | tf_op jit(solution)/shard_map/ppermute | solution.py:253
  87.5 32.3 %collective-permute-start.9 = (f32[2,256,256]{2,1,0:T(8,128)}, f32[2,256,256]{2,1,0:T(8,128)S(1)}, u32[]{:S(2)}, u32[]{:S(2)}) collective-permute-start(f32[2,256,256]{2,1,0:T(8,128)} %get-tuple-element.12), channel_id=1, source_target_pairs={{0,1},{1,2},{2,3},{3,4},{4,5},{5,6},{6,7},{7,8},{8,9},{9,10},{10,1... | collective-permute-start | bytes 1572872 | tf_op jit(solution)/shard_map/ppermute | solution.py:23
  88.8 58.3 %collective-permute-start.8 = (f32[2,512,256]{2,1,0:T(8,128)}, f32[2,512,256]{2,1,0:T(8,128)S(1)}, u32[]{:S(2)}, u32[]{:S(2)}) collective-permute-start(f32[2,512,256]{2,1,0:T(8,128)} %get-tuple-element.10), channel_id=1, source_target_pairs={{0,1},{1,2},{2,3},{3,4},{4,5},{5,6},{6,7},{7,8},{8,9},{9,10},{10,1... | collective-permute-start | bytes 3145736 | tf_op jit(solution)/shard_map/ppermute | solution.py:23
  93.5 4.0 %collective-permute-start.18 = (f32[32,256]{1,0:T(8,128)S(1)}, f32[32,256]{1,0:T(8,128)S(1)}, u32[]{:S(2)}, u32[]{:S(2)}) collective-permute-start(f32[32,256]{1,0:T(8,128)S(1)} %add_add_fusion.1), channel_id=1, source_target_pairs={{0,24},{1,25},{32,56},{33,57},{64,88},{65,89},{96,120},{97,121},{1... | collective-permute-start | bytes 98312 | tf_op jit(solution)/shard_map/ppermute | solution.py:253
  93.6 17.1 %collective-permute-start.17 = (f32[32,256]{1,0:T(8,128)S(1)}, f32[32,256]{1,0:T(8,128)S(1)}, u32[]{:S(2)}, u32[]{:S(2)}) collective-permute-start(f32[32,256]{1,0:T(8,128)S(1)} %add_add_fusion.1), channel_id=1, source_target_pairs={{0,16},{1,17},{32,48},{33,49},{64,80},{65,81},{96,112},{97,113},{1... | collective-permute-start | bytes 98312 | tf_op jit(solution)/shard_map/ppermute | solution.py:253
  93.7 17.0 %collective-permute-start.16 = (f32[32,256]{1,0:T(8,128)S(1)}, f32[32,256]{1,0:T(8,128)S(1)}, u32[]{:S(2)}, u32[]{:S(2)}) collective-permute-start(f32[32,256]{1,0:T(8,128)S(1)} %add_add_fusion.1), channel_id=1, source_target_pairs={{0,8},{1,9},{32,40},{33,41},{64,72},{65,73},{96,104},{97,105},{128... | collective-permute-start | bytes 98312 | tf_op jit(solution)/shard_map/ppermute | solution.py:253
  111.4 15.6 %all-to-all-start.1 = ((f32[8,32,256]{2,1,0:T(8,128)}), f32[8,32,256]{2,1,0:T(8,128)S(1)}, u32[]{:S(2)}, u32[]{:S(2)}) async-start(f32[8,32,256]{2,1,0:T(8,128)} %broadcast_in_dim.3), calls=%async_computation.1 | async-start | bytes 524288 | tf_op jit(solution)/shard_map/all_to_all | solution.py:263
  116.2 19.8 %collective-permute-start.11 = (f32[2,256,256]{2,1,0:T(8,128)}, f32[2,256,256]{2,1,0:T(8,128)S(1)}, u32[]{:S(2)}, u32[]{:S(2)}) collective-permute-start(f32[2,256,256]{2,1,0:T(8,128)} %get-tuple-element.13), channel_id=1, source_target_pairs={{0,16},{16,32},{32,48},{48,64},{64,80},{80,96},{96,112},{112,128},... | collective-permute-start | bytes 1572872 | tf_op jit(solution)/shard_map/ppermute | solution.py:23
  119.8 27.2 %collective-permute-start.10 = (f32[2,256,256]{2,1,0:T(8,128)S(1)}, f32[2,256,256]{2,1,0:T(8,128)S(1)}, u32[]{:S(2)}, u32[]{:S(2)}) collective-permute-start(f32[2,256,256]{2,1,0:T(8,128)S(1)} %add.29), channel_id=1, source_target_pairs={{0,16},{16,32},{32,48},{48,64},{64,80},{80,96},{96,112},{112,128},... | collective-permute-start | bytes 1572872 | tf_op jit(solution)/shard_map/ppermute | solution.py:23
  127.0 25.4 %collective-permute-start.19 = (f32[256,256]{1,0:T(8,128)S(1)}, f32[256,256]{1,0:T(8,128)S(1)}, u32[]{:S(2)}, u32[]{:S(2)}) collective-permute-start(f32[256,256]{1,0:T(8,128)S(1)} %bitcast.7), channel_id=1, source_target_pairs={{0,1},{1,0},{32,33},{33,32},{64,65},{65,64},{96,97},{97,96},{128,1... | collective-permute-start | bytes 786440 | tf_op jit(solution)/shard_map/ppermute | solution.py:253
  136.0 11.0 %copy-start.2 = (f32[2,256,256]{2,1,0:T(8,128)}, f32[2,256,256]{2,1,0:T(8,128)S(1)}, u32[]{:S(2)}) copy-start(f32[2,256,256]{2,1,0:T(8,128)S(1)} %collective-permute-done.11.above1_ref) | copy-start | bytes 1572868
  (5 other events, 15.4 us)
